TPU v7x, 1024 devices: a whole 4x8x16 slice. The times are simulated.
1024 devices in a mesh: blk: 32 (over z, core), col: 32 (over y, x).
Axes of the slice: x: 4, y: 8, z: 16, core: 2. Of those that a mesh axis runs over, the one named last changes fastest.
Arguments:
- three_center: bfloat16 [256, 128, 4, 128], P('blk'), may hold values from -6 to 6
- block_rows: int32 [256], P('blk'), may hold values from 0 to 31, as said below
- occupied: bfloat16 [4096, 4096], P('blk', 'col'), may hold values from -0.1875 to 0.1875
- virtual: bfloat16 [4096, 4096], P('blk'), may hold values from -0.5 to 0.5
Outputs:
- transformed: bfloat16 [4096, 16384], P('blk', 'col')
- response: float32 [4, 4], replicated
Inputs may be any that keep to these rules, and one draw needn't show every extreme that they name: `block_rows`: the 8 entries of each index of blk are distinct.
All inputs are finite; a program needn't handle non-finite values.
Results may differ from a plain program's by a relative error of at most 0.0049.
Values may be sent and summed in bfloat16 or wider, within the bound.
A program may use at most 32 MiB of HBM per device.

v0:
```python
import math

import jax
import jax.numpy as jnp
from jax import lax
from jax.sharding import PartitionSpec as P


def per_device(three_center, block_rows, occupied, virtual):
    block_count, block_size, aux_width, _ = three_center.shape
    strip_width = occupied.shape[1]
    flat_blocks = three_center.reshape(block_count, block_size, aux_width * block_size)
    contract_first = (((0,), (0,)), ((), ()))
    gathered = lax.all_gather(occupied, "blk", axis=0, tiled=True)
    running = jnp.zeros((strip_width, aux_width * block_size), jnp.float32)
    for index in range(block_count):
        occ_rows = lax.dynamic_slice_in_dim(gathered, block_rows[index] * block_size, block_size, 0)
        running = running + lax.dot_general(
            occ_rows, flat_blocks[index], contract_first, preferred_element_type=jnp.float32
        )
    rounded = running.astype(jnp.bfloat16).reshape(strip_width, aux_width, block_size)
    rounded = rounded.transpose(2, 0, 1).reshape(block_size, strip_width * aux_width)
    summed = lax.psum_scatter(
        lax.dot_general(virtual, rounded, contract_first, preferred_element_type=jnp.float32),
        "blk",
        scatter_dimension=0,
        tiled=True,
    )
    transformed = summed.astype(jnp.bfloat16)
    column_index = lax.axis_index("col")
    strip_blocks = strip_width // block_size
    onehot = (
        block_rows[:, None] == column_index * strip_blocks + jnp.arange(strip_blocks)[None, :]
    ).astype(jnp.bfloat16)
    selected = jnp.einsum(
        "kc,klqs->clqs", onehot, three_center, preferred_element_type=jnp.float32
    ).astype(jnp.bfloat16)
    doubly_tile = transformed.reshape(block_size, strip_blocks, block_size, aux_width)
    partial_value = jnp.einsum(
        "sclp,clqs->pq", doubly_tile, selected, preferred_element_type=jnp.float32
    )
    response = lax.psum(partial_value, ("blk", "col"))
    response = response / (block_size * math.sqrt(lax.axis_size("blk") * block_count))
    return (transformed, response)


def solution(mesh):
    in_specs = (P("blk", None, None, None), P("blk"), P("blk", "col"), P("blk", None))
    out_specs = (P("blk", "col"), P())
    return jax.shard_map(
        per_device, mesh=mesh, in_specs=in_specs, out_specs=out_specs, check_vma=False
    )
```

profile of v0, /device:TPU:1, one launch (start us, length us, event | category | flops | bytes accessed | tf_op | source)
XLA Modules:
  0.0 358.7 jit_solution(16100993610262652742)
XLA Ops:
  7.2 0.0 copy-start
  7.2 0.0 all-gather.2.cloned.1.call-start
  7.2 0.7 all-gather.2.cloned.1.call-update
  7.9 0.0 reduce-scatter.2.cloned.1.call-start
  8.0 1.6 fusion.41
  14.6 1.6 fusion.40
  16.2 78.0 %all-gather.2.cloned.1.call-done = bf16[4096,128]{1,0:T(8,128)(2,1)} async-done(((bf16[128,128]{1,0:T(8,128)(2,1)}), bf16[4096,128]{1,0:T(8,128)(2,1)}) %all-gather.2.cloned.1.call-update) | async-done | bytes 1048592 | tf_op jit(solution)/shard_map/all_gather | solution.py:14
  94.3 1.0 fusion.17
  95.2 1.0 convolution_add_fusion.6
  96.2 1.0 convolution_add_fusion.5
  97.2 1.0 convolution_add_fusion.4
  98.2 1.0 convolution_add_fusion.3
  99.2 1.0 convolution_add_fusion.2
  100.1 1.0 convolution_add_fusion.1
  101.1 1.0 fusion
  102.1 0.0 copy-done
  102.1 0.0 copy-start.1
  102.1 0.0 copy-start.2
  102.2 4.5 %convolution_bitcast_fusion = f32[4096,512]{0,1:T(8,128)} fusion(bf16[128,512]{0,1:T(8,128)(2,1)S(1)} %bitcast.66, bf16[128,4096]{1,0:T(8,128)(2,1)S(1)} %copy-done), kind=kOutput, calls=%fused_computation | convolution fusion | flops 536870912 | bytes 9568256 | tf_op jit(solution)/shard_map/dot_general | solution.py:24
  106.6 0.0 reduce-scatter.2.cloned.1.call-update
  106.7 0.0 copy-done.1
  106.7 0.0 copy-done.2
  106.7 0.7 fusion.1
  107.4 117.5 %reduce-scatter.2.cloned.1.call-done = f32[128,512]{0,1:T(8,128)} async-done(((f32[4096,512]{0,1:T(8,128)}), f32[128,512]{0,1:T(8,128)}) %reduce-scatter.2.cloned.1.call-update) | async-done | bytes 262160 | tf_op jit(solution)/shard_map/reduce_scatter | solution.py:23
  225.0 1.0 convert_element_type.12
  225.9 0.3 convolution_bitcast_fusion.1
  226.2 0.8 copy.6
  227.0 124.3 %psum.7 = f32[4,4]{1,0:T(4,128)S(1)} all-reduce(f32[4,4]{1,0:T(4,128)S(1)} %convolution_bitcast_fusion.1), channel_id=1, replica_groups=mesh['blk'=32,'col'=32] {'blk','col'}, use_global_device_ids=true, to_apply=%region_1.0 | all-reduce | flops 16 | bytes 128 | tf_op jit(solution)/shard_map/psum | solution.py:42
  351.3 0.6 broadcast_multiply_fusion
  (1 shorter events, 0.0 us)
Async XLA Ops:
  7.2 95.0 %copy-start = (bf16[128,4096]{1,0:T(8,128)(2,1)S(1)}, bf16[128,4096]{1,0:T(8,128)(2,1)}, u32[]{:S(2)}) copy-start(bf16[128,4096]{1,0:T(8,128)(2,1)} %param.7) | copy-start | bytes 3145732
  7.2 87.1 %all-gather.2.cloned.1.call-start = ((), (), s32[]{:S(2)}) async-start(), calls=%async_computation.1 | async-start | bytes 1081344 | tf_op jit(solution)/shard_map/all_gather | solution.py:14
  7.9 217.0 %reduce-scatter.2.cloned.1.call-start = ((), (), s32[]{:S(2)}) async-start(), calls=%async_computation.2 | async-start | bytes 8650752 | tf_op jit(solution)/shard_map/reduce_scatter | solution.py:23
  102.1 4.5 %copy-start.1 = (bf16[8,128,4,128]{3,2,1,0:T(4,128)(2,1)S(1)}, bf16[8,128,4,128]{3,2,1,0:T(4,128)(2,1)}, u32[]{:S(2)}) copy-start(bf16[8,128,4,128]{3,2,1,0:T(4,128)(2,1)} %param.4) | copy-start | bytes 3145732
  102.1 4.5 %copy-start.2 = (s32[8]{0:T(128)S(1)}, s32[8]{0:T(128)}, u32[]{:S(2)}) copy-start(s32[8]{0:T(128)} %param.5) | copy-start | bytes 100
Sparse Core Ops, SparseCore 0:
  10.7 83.5 all-gather.1
  106.8 118.1 reduce-scatter.1
where the time goes:
time: 360 us; the launch traced here: 359 us
  waiting for transfers between devices  196 us (54%)
  blocking collectives  124 us (34%)
  between operations  19.2 us (5%)
  matrix products  13.2 us (4%)
  local copies, waits for them, and re-layouts  4.11 us (1%)
    psum x1, blocking collectives, per_device(): response = lax.psum(partial_value, ('blk', 'col'))  124 us
    reduce_scatter x1, waiting for transfers between devices, per_device(): lax.psum_scatter(lax.dot_general(virtual, rounded, contract_first, prefer...  118 us
    all_gather x1, waiting for transfers between devices, per_device(): gathered = lax.all_gather(occupied, 'blk', axis=0, tiled=True)  78 us
    dot_general x8, matrix products, per_device(): lax.dot_general(occ_rows, flat_blocks[index], contract_first, preferred_e...  7.75 us
  transfers between devices with their start and end apart: 2, of which 2 were waited for; matrix products, arithmetic and copies ran while one was open for 1% of the time, Pallas kernels for 0%

commit v1 on v0

v1 whole, which is shorter than its diff:
```python
import functools
import math

import jax
import jax.numpy as jnp
from jax import lax
from jax.experimental import pallas as pl
from jax.experimental.pallas import tpu as pltpu
from jax.sharding import PartitionSpec as P

BS = 128
AUX = 4
CORES = 2
DIMS = (16, 8, 4)
MESH = pl.DeviceIdType.MESH


def kernel(
    dims, rows_ref, blocks_hbm, occ_hbm, virt_hbm, out_ref, resp_ref,
    occ_in, blocks_in, perm, blocks, chosen, occ_all, s_all, virt_all, acc, sum_z, sum_y, sum_x,
    in_sem, o_send, o_recv, op_send, op_recv, s_send, s_recv, sp_send, sp_recv,
    vz_send, vz_recv, vx_send, vx_recv, vy_send, vy_recv,
    rz_send, rz_recv, ry_send, ry_recv, rx_send, rx_recv,
):
    nz, ny, nx = dims
    nb = CORES * nz
    n_stored = blocks.shape[0] // BS
    share = BS // ny
    n_part = nb // nx
    half_z, half_y = nz // 2, ny // 2

    blk, col = lax.axis_index("blk"), lax.axis_index("col")
    z, core = lax.div(blk, CORES), lax.rem(blk, CORES)
    y, x = lax.div(col, nx), lax.rem(col, nx)

    def wrap(value, size):
        return lax.rem(value + 2 * size, size)

    def at_z(step, which=None):
        which = core if which is None else which
        return wrap(z + step, nz) * CORES + which

    right, left = (at_z(1), col), (at_z(-1), col)
    pair = (z * CORES + 1 - core, col)
    up, down = (blk, wrap(y + 1, ny) * nx + x), (blk, wrap(y - 1, ny) * nx + x)

    load_occ = pltpu.make_async_copy(occ_hbm, occ_in, in_sem.at[0])
    load_blocks = pltpu.make_async_copy(blocks_hbm, blocks_in, in_sem.at[1])
    load_occ.start()
    load_blocks.start()

    barrier = pltpu.get_barrier_semaphore()

    def greet(blk_to, col_to):
        pl.semaphore_signal(barrier, inc=1, device_id=(blk_to, col_to), device_id_type=MESH)

    @pl.loop(1, nb)
    def _(step):
        greet(wrap(blk + step, nb), col)

    @pl.loop(1, ny)
    def _(step):
        greet(blk, wrap(y + step, ny) * nx + x)

    @pl.loop(1, nx)
    def _(step):
        greet(z * CORES, y * nx + wrap(x + step, nx))
        greet(z * CORES + 1, y * nx + wrap(x + step, nx))

    load_occ.wait()
    occ_all[blk] = occ_in[...].T
    pl.semaphore_wait(barrier, (nb - 1) + (ny - 1) + CORES * (nx - 1))

    sent = []

    def send(src, dst, send_sem, recv_sem, to):
        copy = pltpu.make_async_remote_copy(
            src_ref=src, dst_ref=dst, send_sem=send_sem, recv_sem=recv_sem, device_id=to, device_id_type=MESH
        )
        copy.start()
        sent.append(copy)

    def arrive(ref, send_sem, recv_sem, source):
        pltpu.make_async_remote_copy(
            src_ref=ref, dst_ref=ref, send_sem=send_sem, recv_sem=recv_sem, device_id=source, device_id_type=MESH
        ).wait_recv()

    def occ_view(way, step, which=None):
        index = at_z(-step if way == 0 else step, which)
        return occ_all.at[index]

    def occ_half(way, which=None):
        index = at_z(half_z, which)
        return occ_all.at[index, pl.ds(way * (BS // 2), BS // 2)]

    def occ_forward(way, step):
        to = right if way == 0 else left
        if step + 1 < half_z:
            view = occ_view(way, step)
        else:
            index = at_z(-step if way == 0 else step)
            view = occ_all.at[index, pl.ds(way * (BS // 2), BS // 2)]
        send(view, view, o_send.at[way, step + 1], o_recv.at[way, step + 1], to)

    def occ_pair(way, step):
        view = occ_view(way, step) if step < half_z else occ_half(way)
        send(view, view, op_send.at[way, step], op_recv.at[way, step], pair)

    def occ_arrive(way, step):
        view = occ_view(way, step) if step < half_z else occ_half(way)
        arrive(view, o_send.at[way, step], o_recv.at[way, step], left if way == 0 else right)

    def occ_pair_arrive(way, step):
        view = occ_view(way, step, 1 - core) if step < half_z else occ_half(way, 1 - core)
        arrive(view, op_send.at[way, step], op_recv.at[way, step], pair)

    occ_forward(0, 0)
    occ_forward(1, 0)
    occ_pair(0, 0)

    def virt_part(part):
        return virt_all.at[y, x, part]

    def virt_source(to):
        return virt_hbm.at[pl.ds(y * share, share), pl.ds(pl.multiple_of(to * BS, BS), BS)]

    def virt_remote(part):
        to = wrap(blk + x + nx * part, nb)
        return pltpu.make_async_remote_copy(
            src_ref=virt_source(to), dst_ref=virt_part(part), send_sem=vz_send.at[part], recv_sem=vz_recv.at[part],
            device_id=(to, col), device_id_type=MESH,
        )

    def virt_local():
        return pltpu.make_async_copy(virt_source(blk), virt_part(0), vz_recv.at[0])

    @pl.when(x != 0)
    def _():
        virt_remote(0).start()

    @pl.when(x == 0)
    def _():
        virt_local().start()

    for part in range(1, n_part):
        virt_remote(part).start()

    row = lax.broadcasted_iota(jnp.int32, (AUX * BS, AUX * BS), 0)
    column = lax.broadcasted_iota(jnp.int32, (AUX * BS, AUX * BS), 1)
    perm[...] = (column == (row & (BS - 1)) * AUX + (row >> 7)).astype(jnp.float32).astype(jnp.bfloat16)
    load_blocks.wait()

    def order_blocks(index):
        rows = pl.ds(index * AUX * BS, AUX * BS)
        ordered = jnp.dot(perm[...], blocks_in[rows, :], preferred_element_type=jnp.float32).astype(jnp.bfloat16)
        for aux in range(AUX):
            blocks[pl.ds(index * BS, BS), pl.ds(aux * BS, BS)] = ordered[aux * BS:(aux + 1) * BS, :]

    def virt_arrived():
        @pl.when(x != 0)
        def _():
            virt_remote(0).wait()

        @pl.when(x == 0)
        def _():
            virt_local().wait()

        for part in range(1, n_part):
            virt_remote(part).wait()
        for step in range(1, nx):
            send(virt_all.at[y, x], virt_all.at[y, x], vx_send.at[step], vx_recv.at[step],
                 (blk, y * nx + wrap(x + step, nx)))

    def virt_y_send(way, step):
        to = up if way == 0 else down
        index = wrap(y - step if way == 0 else y + step, ny)
        if step + 1 < half_y:
            view = virt_all.at[index]
        else:
            view = virt_all.at[index, pl.ds(way * (nx // 2), nx // 2)]
        send(view, view, vy_send.at[way, step + 1], vy_recv.at[way, step + 1], to)

    def virt_y_arrive(way, step):
        index = wrap(y - step if way == 0 else y + step, ny)
        if step < half_y:
            view = virt_all.at[index]
        else:
            view = virt_all.at[index, pl.ds(way * (nx // 2), nx // 2)]
        arrive(view, vy_send.at[way, step], vy_recv.at[way, step], down if way == 0 else up)

    def virt_x_arrived():
        for step in range(1, nx):
            source = wrap(x - step, nx)
            arrive(virt_all.at[y, source], vx_send.at[step], vx_recv.at[step], (blk, y * nx + source))
        virt_y_send(0, 0)
        virt_y_send(1, 0)

    order_blocks(0)
    for step in range(1, half_z + 1):
        for way in (0, 1):
            occ_arrive(way, step)
            if step < half_z:
                occ_forward(way, step)
            occ_pair(way, step)
        if step < n_stored:
            order_blocks(step)
        if step == half_z // 2:
            virt_arrived()
    for index in range(half_z + 1, n_stored):
        order_blocks(index)
    virt_x_arrived()
    occ_pair_arrive(0, 0)
    for step in range(1, half_z + 1):
        for way in (0, 1):
            occ_pair_arrive(way, step)

    def s_view(way, step, sub, which=None):
        return s_all.at[at_z(-step if way == 0 else step, which), pl.ds(2 * sub, 2)]

    def s_forward(way, step, sub):
        if step + 1 < half_z or sub == way:
            view = s_view(way, step, sub)
            send(view, view, s_send.at[way, step + 1, sub], s_recv.at[way, step + 1, sub], right if way == 0 else left)

    def s_pair(way, step, sub):
        view = s_view(way, step, sub)
        send(view, view, sp_send.at[way, step, sub], sp_recv.at[way, step, sub], pair)

    def s_arrive(way, step, sub):
        arrive(s_view(way, step, sub), s_send.at[way, step, sub], s_recv.at[way, step, sub],
               left if way == 0 else right)

    def s_pair_arrive(way, step, sub):
        arrive(s_view(way, step, sub, 1 - core), sp_send.at[way, step, sub], sp_recv.at[way, step, sub], pair)

    occ_rows = jnp.concatenate([occ_all[rows_ref[index]] for index in range(n_stored)], axis=1)
    for sub in (0, 1):
        sums = jnp.dot(
            occ_rows, blocks[:, sub * 2 * BS:(sub + 1) * 2 * BS], preferred_element_type=jnp.float32
        ).astype(jnp.bfloat16)
        for aux in (0, 1):
            s_all[blk, 2 * sub + aux] = sums[:, aux * BS:(aux + 1) * BS]
        s_forward(0, 0, sub)
        s_forward(1, 0, sub)
        s_pair(0, 0, sub)

    picked = jnp.zeros((BS, AUX * BS), jnp.float32)
    for index in range(n_stored):
        here = (rows_ref[index] == col).astype(jnp.float32)
        picked = picked + blocks[index * BS:(index + 1) * BS, :].astype(jnp.float32) * here
    chosen[...] = picked

    def contribute(way, step, sub, first=False):
        base = wrap(z - step if way == 0 else z + step, nz)
        pieces, rows = [], []
        for which in range(CORES):
            index = base * CORES + which
            pieces.append(s_all[index, 2 * sub:2 * sub + 2].reshape(2 * BS, BS))
            away = wrap(blk - index, nb)
            rows.append(virt_all[:, lax.rem(away, nx), lax.div(away, nx)].reshape(BS, BS))
        term = jnp.dot(
            jnp.concatenate(pieces, axis=1), jnp.concatenate(rows, axis=0), preferred_element_type=jnp.float32
        )
        where = pl.ds(sub * 2 * BS, 2 * BS)
        acc[where, :] = term if first else acc[where, :] + term

    def contribute_step(step):
        if step == 0:
            for sub in (0, 1):
                s_pair_arrive(0, 0, sub)
                contribute(0, 0, sub, first=True)
        else:
            for sub in (0, 1):
                for way in (0, 1):
                    if step < half_z or sub == way:
                        s_pair_arrive(way, step, sub)
                        contribute(way, step, sub)

    done = 0
    for step in range(1, half_z + 1):
        for sub in (0, 1):
            for way in (0, 1):
                if step < half_z or sub == way:
                    s_arrive(way, step, sub)
                    if step < half_z:
                        s_forward(way, step, sub)
                    s_pair(way, step, sub)
        if step <= half_y:
            for way in (0, 1):
                virt_y_arrive(way, step)
                if step < half_y:
                    virt_y_send(way, step)
        if step >= half_y:
            for _ in range(2):
                if done < step:
                    contribute_step(done)
                    done += 1
    while done <= half_z:
        contribute_step(done)
        done += 1

    rounded = acc[...].astype(jnp.bfloat16)
    tiles = rounded.astype(jnp.float32)
    lane = lax.broadcasted_iota(jnp.int32, (1, BS), 1)
    message = jnp.zeros((1, BS), jnp.float32)
    for first in range(AUX):
        tile = tiles[first * BS:(first + 1) * BS, :]
        for second in range(AUX):
            product = tile * chosen[:, second * BS:(second + 1) * BS]
            total = jnp.sum(jnp.sum(product, axis=0, keepdims=True), axis=1, keepdims=True)
            message = message + jnp.where(lane == first * AUX + second, total, 0.0)

    def exchange(buffer, mine, members, send_sem, recv_sem, device_of, value):
        buffer[mine] = value

        def copy_to(step, slot):
            return pltpu.make_async_remote_copy(
                src_ref=buffer.at[slot], dst_ref=buffer.at[slot], send_sem=send_sem.at[step],
                recv_sem=recv_sem.at[slot], device_id=device_of(wrap(mine + step, members)), device_id_type=MESH,
            )

        @pl.loop(1, members)
        def _(step):
            copy_to(step, mine).start()

        def collect():
            @pl.loop(1, members)
            def _(step):
                copy_to(step, wrap(mine + step, members)).wait_recv()

            @pl.loop(1, members)
            def _(step):
                copy_to(step, mine).wait_send()

            return jnp.sum(buffer[...], axis=0)

        return collect

    collect = exchange(sum_z, z, nz, rz_send, rz_recv, lambda to: (to * CORES + core, col), message)
    out_ref[...] = lax.dot_general(
        rounded, perm[...], (((0,), (0,)), ((), ())), preferred_element_type=jnp.float32
    ).astype(jnp.bfloat16)
    message = collect()
    message = exchange(sum_y, y, ny, ry_send, ry_recv, lambda to: (blk, to * nx + x), message)()
    message = exchange(
        sum_x, core * nx + x, CORES * nx, rx_send, rx_recv,
        lambda to: (z * CORES + lax.div(to, nx), y * nx + lax.rem(to, nx)), message,
    )()

    scale = 1.0 / (BS * math.sqrt(nb * n_stored))
    value = jnp.broadcast_to(message, (AUX, BS)) * scale
    lanes = lax.broadcasted_iota(jnp.int32, (AUX, BS), 1)
    firsts = lax.broadcasted_iota(jnp.int32, (AUX, BS), 0)
    place = lax.broadcasted_iota(jnp.int32, (AUX, AUX), 1)
    response = jnp.zeros((AUX, AUX), jnp.float32)
    for second in range(AUX):
        picked = jnp.sum(jnp.where(lanes == firsts * AUX + second, value, 0.0), axis=1, keepdims=True)
        response = response + jnp.where(place == second, picked, 0.0)
    resp_ref[...] = response

    for copy in sent:
        copy.wait_send()


def per_device(dims, three_center, block_rows, occupied, virtual):
    nz, ny, nx = dims
    nb = CORES * nz
    n_stored = three_center.shape[0]
    half_z, half_y = nz // 2, ny // 2
    any_space = pl.BlockSpec(memory_space=pl.ANY)
    vmem = pl.BlockSpec(memory_space=pltpu.VMEM)
    bf16, f32 = jnp.bfloat16, jnp.float32
    dma = pltpu.SemaphoreType.DMA
    return pl.pallas_call(
        functools.partial(kernel, dims),
        out_shape=(
            jax.ShapeDtypeStruct((BS, AUX * BS), bf16),
            jax.ShapeDtypeStruct((AUX, AUX), f32),
        ),
        in_specs=[pl.BlockSpec(memory_space=pltpu.SMEM), any_space, any_space, any_space],
        out_specs=(vmem, vmem),
        scratch_shapes=[
            pltpu.VMEM((BS, BS), bf16),
            pltpu.VMEM((n_stored * BS * AUX, BS), bf16),
            pltpu.VMEM((AUX * BS, AUX * BS), bf16),
            pltpu.VMEM((n_stored * BS, AUX * BS), bf16),
            pltpu.VMEM((BS, AUX * BS), f32),
            pltpu.VMEM((nb, BS, BS), bf16),
            pltpu.VMEM((nb, AUX, BS, BS), bf16),
            pltpu.VMEM((ny, nx, nb // nx, BS // ny, BS), bf16),
            pltpu.VMEM((AUX * BS, BS), f32),
            pltpu.VMEM((nz, 1, BS), f32),
            pltpu.VMEM((ny, 1, BS), f32),
            pltpu.VMEM((CORES * nx, 1, BS), f32),
            dma((2,)),
            dma((2, half_z + 1)), dma((2, half_z + 1)),
            dma((2, half_z + 1)), dma((2, half_z + 1)),
            dma((2, half_z + 1, 2)), dma((2, half_z + 1, 2)),
            dma((2, half_z + 1, 2)), dma((2, half_z + 1, 2)),
            dma((nb // nx,)), dma((nb // nx,)),
            dma((nx,)), dma((nx,)),
            dma((2, half_y + 1)), dma((2, half_y + 1)),
            dma((nz,)), dma((nz,)),
            dma((ny,)), dma((ny,)),
            dma((CORES * nx,)), dma((CORES * nx,)),
        ],
        compiler_params=pltpu.CompilerParams(
            collective_id=0, has_side_effects=True, vmem_limit_bytes=32 * 1024 * 1024
        ),
    )(block_rows, three_center.reshape(-1, BS), occupied, virtual)


def solution(mesh):
    in_specs = (P("blk", None, None, None), P("blk"), P("blk", "col"), P("blk", None))
    out_specs = (P("blk", "col"), P())
    return jax.shard_map(
        functools.partial(per_device, DIMS), mesh=mesh, in_specs=in_specs, out_specs=out_specs, check_vma=False
    )
```

time: 360 us -> 110 us (0.31)
  waiting for transfers between devices: 196 us -> 0 us
  blocking collectives: 124 us -> 0 us
  Pallas kernels: 0 us -> 104 us
  between operations: 19.2 us -> 0.65 us
  matrix products: 13.2 us -> 0 us
    psum x1 -> x0, blocking collectives: 124 us -> none  [per_device(): response = lax.psum(partial_value, ('blk', 'col'))]
    reduce_scatter x1 -> x0, waiting for transfers between devices: 118 us -> none  [per_device(): lax.psum_scatter(lax.dot_general(virtual, rounded, contract_first, prefer...]
    pallas_call x0 -> x1, Pallas kernels: none -> 104 us  [per_device(): pl.pallas_call(functools.partial(kernel, dims), out_shape=(jax.ShapeDtype...]
    all_gather x1 -> x0, waiting for transfers between devices: 78 us -> none  [per_device(): gathered = lax.all_gather(occupied, 'blk', axis=0, tiled=True)]
    dot_general x11 -> x0, matrix products: 13.2 us -> none  [the longest x8 7.75 us: per_device(): lax.dot_general(occ_rows, flat_blocks[index], contract_first, preferred_e...]
    unnamed x7 -> x10, local copies, waits for them, and re-layouts: 0.81 us -> 5.09 us
  transfers between devices with their start and end apart: 2 -> 0, of which waited for: 2 -> 0; matrix products, arithmetic and copies ran while one was open for 1% -> 0% of each run, Pallas kernels for 0% -> 0%
where the time goes in v1:
time: 110 us
  Pallas kernels  104 us (95%)
  local copies, waits for them, and re-layouts  5.09 us (5%)
    pallas_call x1, Pallas kernels, per_device(): pl.pallas_call(functools.partial(kernel, dims), out_shape=(jax.ShapeDtype...  104 us
    unnamed x10, local copies, waits for them, and re-layouts  5.09 us

profile of v1, /device:TPU:1, one launch (start us, length us, event | category | flops | bytes accessed | tf_op | source)
XLA Modules:
  0.0 109.8 jit_solution(7282755586789369717)
XLA Ops:
  0.6 0.0 copy-start.3
  0.6 0.6 copy-done.3
  1.3 0.0 copy-start
  1.3 1.2 %copy-done = bf16[8,128,4,128]{3,2,1,0:T(4,128)(2,1)S(1)} copy-done((bf16[8,128,4,128]{3,2,1,0:T(4,128)(2,1)S(1)}, bf16[8,128,4,128]{3,2,1,0:T(4,128)(2,1)}, u32[]{:S(2)}) %copy-start) | copy-done | bytes 1048600
  2.5 0.0 copy-start.1
  2.5 1.2 %copy-done.1 = bf16[128,4096]{1,0:T(8,128)(2,1)S(1)} copy-done((bf16[128,4096]{1,0:T(8,128)(2,1)S(1)}, bf16[128,4096]{1,0:T(8,128)(2,1)}, u32[]{:S(2)}) %copy-start.1) | copy-done | bytes 1048600
  3.7 0.0 copy-start.2
  3.7 0.8 copy-done.2
  4.5 104.0 %shard_map.59 = (bf16[128,512]{1,0:T(8,128)(2,1)S(1)}, f32[4,4]{1,0:T(4,128)S(1)}) custom-call(s32[8]{0:T(128)S(1)} %copy-done.3, bf16[4096,128]{1,0:T(8,128)(2,1)S(1)} %bitcast.1, bf16[128,128]{1,0:T(8,128)(2,1)S(1)} %copy-done.2, bf16[128,4096]{1,0:T(8,128)(2,1)S(1)} %copy-done.1), custom_call_target="tpu_custom_call" | custom-call | tf_op jit(solution)/shard_map/pallas_call | solution.py:374
  108.5 0.7 copy.8
  109.2 0.6 copy.9
Async XLA Ops:
  0.6 0.7 copy-start.3
  1.3 1.2 %copy-start = (bf16[8,128,4,128]{3,2,1,0:T(4,128)(2,1)S(1)}, bf16[8,128,4,128]{3,2,1,0:T(4,128)(2,1)}, u32[]{:S(2)}) copy-start(bf16[8,128,4,128]{3,2,1,0:T(4,128)(2,1)} %param.4) | copy-start | bytes 3145732
  2.5 1.2 %copy-start.1 = (bf16[128,4096]{1,0:T(8,128)(2,1)S(1)}, bf16[128,4096]{1,0:T(8,128)(2,1)}, u32[]{:S(2)}) copy-start(bf16[128,4096]{1,0:T(8,128)(2,1)} %virt_hbm.1) | copy-start | bytes 3145732
  3.7 0.8 copy-start.2

commit v2 on v1

v2 whole, which is shorter than its diff:
```python
import functools
import math

import jax
import jax.numpy as jnp
from jax import lax
from jax.experimental import pallas as pl
from jax.experimental.pallas import tpu as pltpu
from jax.sharding import PartitionSpec as P

BS = 128
AUX = 4
CORES = 2
DIMS = (16, 8, 4)
MESH = pl.DeviceIdType.MESH
V_STEP = 2
OCC_FROM = {1: 0, 2: 0, 3: 0, 4: 3, 5: 3, 6: 3, 7: 6, 8: 6}


def kernel(
    dims, rows_ref, blocks_hbm, occ_hbm, virt_hbm, out_ref, resp_ref,
    occ_in, blocks_in, wide, blocks, chosen, occ_all, s_all, virt_all, acc, spread, sum_z, sum_c,
    in_sem, o_send, o_recv, op_send, op_recv, s_send, s_recv, sp_send, sp_recv,
    vz_send, vz_recv, vx_send, vx_recv, vy_send, vy_recv, r_send, r_recv,
):
    nz, ny, nx = dims
    nb = CORES * nz
    n_stored = blocks.shape[0] // BS
    share = BS // ny
    n_part = nb // nx
    half_z, half_y = nz // 2, ny // 2

    blk, col = lax.axis_index("blk"), lax.axis_index("col")
    z, core = lax.div(blk, CORES), lax.rem(blk, CORES)
    y, x = lax.div(col, nx), lax.rem(col, nx)

    def wrap(value, size):
        return lax.rem(value + 2 * size, size)

    def at_z(step, which=None):
        which = core if which is None else which
        return wrap(z + step, nz) * CORES + which

    right, left = (at_z(1), col), (at_z(-1), col)
    pair = (z * CORES + 1 - core, col)
    up, down = (blk, wrap(y + 1, ny) * nx + x), (blk, wrap(y - 1, ny) * nx + x)

    load_occ = pltpu.make_async_copy(occ_hbm, occ_in, in_sem.at[0])
    load_blocks = pltpu.make_async_copy(blocks_hbm, blocks_in, in_sem.at[1])
    load_occ.start()
    load_blocks.start()

    barrier = pltpu.get_barrier_semaphore()
    near_z = [hops for hops in sorted({reach - start for reach, start in OCC_FROM.items()}) if hops <= half_z]
    greeted = [(at_z(sign * hops), col) for hops in near_z for sign in (1, -1)] + [pair, up, down]
    greeted += [(blk, y * nx + wrap(x + step, nx)) for step in range(1, nx)]
    for device in greeted:
        pl.semaphore_signal(barrier, inc=1, device_id=device, device_id_type=MESH)
    load_occ.wait()
    occ_all[blk] = occ_in[...].T
    pl.semaphore_wait(barrier, len(greeted))

    def send(src, dst, send_sem, recv_sem, to):
        copy = pltpu.make_async_remote_copy(
            src_ref=src, dst_ref=dst, send_sem=send_sem, recv_sem=recv_sem, device_id=to, device_id_type=MESH
        )
        copy.start()

    def arrive(ref, send_sem, recv_sem, source):
        pltpu.make_async_remote_copy(
            src_ref=ref, dst_ref=ref, send_sem=send_sem, recv_sem=recv_sem, device_id=source, device_id_type=MESH
        ).wait_recv()

    def occ_view(way, step, part, which=None):
        index = at_z(-step if way == 0 else step, which)
        if part < half_z:
            return occ_all.at[index]
        return occ_all.at[index, pl.ds(way * (BS // 2), BS // 2)]

    def occ_forward(way, step):
        for reach in range(half_z, step, -1):
            if OCC_FROM[reach] == step:
                view = occ_view(way, step, reach)
                hops = reach - step
                send(view, view, o_send.at[0], o_recv.at[way, reach], (at_z(hops if way == 0 else -hops), col))

    def occ_pair(way, step):
        view = occ_view(way, step, step)
        send(view, view, op_send.at[0], op_recv.at[way, step], pair)

    def occ_arrive(way, step):
        hops = step - OCC_FROM[step]
        arrive(occ_view(way, step, step), o_send.at[0], o_recv.at[way, step],
               (at_z(-hops if way == 0 else hops), col))

    def occ_pair_arrive(way, step):
        arrive(occ_view(way, step, step, 1 - core), op_send.at[0], op_recv.at[way, step], pair)

    occ_forward(0, 0)
    occ_forward(1, 0)
    occ_pair(0, 0)

    def virt_part(part):
        return virt_all.at[y, x, part]

    def virt_source(to):
        return virt_hbm.at[pl.ds(y * share, share), pl.ds(pl.multiple_of(to * BS, BS), BS)]

    def virt_remote(part):
        to = wrap(blk + x + nx * part, nb)
        return pltpu.make_async_remote_copy(
            src_ref=virt_source(to), dst_ref=virt_part(part), send_sem=vz_send.at[part], recv_sem=vz_recv.at[part],
            device_id=(to, col), device_id_type=MESH,
        )

    def virt_local():
        return pltpu.make_async_copy(virt_source(blk), virt_part(0), vz_recv.at[0])

    def virt_start():
        @pl.when(x != 0)
        def _():
            virt_remote(0).start()

        @pl.when(x == 0)
        def _():
            virt_local().start()

        for part in range(1, n_part):
            virt_remote(part).start()

    load_blocks.wait()

    def order_blocks(index):
        base = index * AUX * BS
        wide[pl.ds(base, AUX * BS), :] = blocks_in[pl.ds(base, AUX * BS), :].astype(jnp.float32)
        for aux in range(AUX):
            blocks[pl.ds(index * BS, BS), pl.ds(aux * BS, BS)] = wide[pl.ds(base + aux, BS, stride=AUX), :].astype(
                jnp.bfloat16
            )

    def virt_arrived():
        @pl.when(x != 0)
        def _():
            virt_remote(0).wait()

        @pl.when(x == 0)
        def _():
            virt_local().wait()

        for part in range(1, n_part):
            virt_remote(part).wait()
        for step in range(1, nx):
            send(virt_all.at[y, x], virt_all.at[y, x], vx_send.at[0], vx_recv.at[step],
                 (blk, y * nx + wrap(x + step, nx)))

    def virt_y_view(way, step, sub):
        return virt_all.at[wrap(y - step if way == 0 else y + step, ny), pl.ds(sub * (nx // 2), nx // 2)]

    def virt_y_send(way, step, sub):
        if step + 1 < half_y or sub == way:
            view = virt_y_view(way, step, sub)
            send(view, view, vy_send.at[0], vy_recv.at[way, step + 1, sub], up if way == 0 else down)

    def virt_y_step(step):
        for sub in (0, 1):
            for way in (0, 1):
                if step < half_y or sub == way:
                    arrive(virt_y_view(way, step, sub), vy_send.at[0], vy_recv.at[way, step, sub],
                           down if way == 0 else up)
                    if step < half_y:
                        virt_y_send(way, step, sub)

    def virt_x_arrived():
        for step in range(1, nx):
            source = wrap(x - step, nx)
            arrive(virt_all.at[y, source], vx_send.at[0], vx_recv.at[step], (blk, y * nx + source))
        for sub in (0, 1):
            virt_y_send(0, 0, sub)
            virt_y_send(1, 0, sub)

    for index in range(n_stored):
        order_blocks(index)
    for step in range(1, half_z + 1):
        for way in (0, 1):
            occ_arrive(way, step)
            if step < half_z:
                occ_forward(way, step)
        for way in (0, 1):
            occ_pair(way, step)
    occ_pair_arrive(0, 0)
    for step in range(1, half_z + 1):
        for way in (0, 1):
            occ_pair_arrive(way, step)

    def s_view(way, step, sub, which=None):
        return s_all.at[at_z(-step if way == 0 else step, which), sub]

    def s_forward(way, step, sub):
        if step + 1 < half_z or sub // 2 == way:
            view = s_view(way, step, sub)
            send(view, view, s_send.at[0], s_recv.at[way, step + 1, sub], right if way == 0 else left)

    def s_pair(way, step, sub):
        view = s_view(way, step, sub)
        send(view, view, sp_send.at[0], sp_recv.at[way, step, sub], pair)

    def s_arrive(way, step, sub):
        arrive(s_view(way, step, sub), s_send.at[0], s_recv.at[way, step, sub],
               left if way == 0 else right)

    def s_pair_arrive(way, step, sub):
        arrive(s_view(way, step, sub, 1 - core), sp_send.at[0], sp_recv.at[way, step, sub], pair)

    occ_rows = jnp.concatenate([occ_all[rows_ref[index]] for index in range(n_stored)], axis=1)
    for half in (0, 1):
        sums = jnp.dot(
            occ_rows, blocks[:, half * 2 * BS:(half + 1) * 2 * BS], preferred_element_type=jnp.float32
        ).astype(jnp.bfloat16)
        for sub in (2 * half, 2 * half + 1):
            s_all[blk, sub] = sums[:, (sub % 2) * BS:(sub % 2 + 1) * BS]
            s_forward(0, 0, sub)
            s_forward(1, 0, sub)
        for sub in (2 * half, 2 * half + 1):
            s_pair(0, 0, sub)
    virt_start()

    picked = jnp.zeros((BS, AUX * BS), jnp.float32)
    for index in range(n_stored):
        here = (rows_ref[index] == col).astype(jnp.float32)
        picked = picked + blocks[index * BS:(index + 1) * BS, :].astype(jnp.float32) * here
    chosen[...] = picked

    def contribute(way, step, half, first=False):
        base = wrap(z - step if way == 0 else z + step, nz)
        pieces, rows = [], []
        for which in range(CORES):
            index = base * CORES + which
            pieces.append(s_all[index, 2 * half:2 * half + 2].reshape(2 * BS, BS))
            away = wrap(blk - index, nb)
            rows.append(virt_all[:, lax.rem(away, nx), lax.div(away, nx)].reshape(BS, BS))
        term = jnp.dot(
            jnp.concatenate(pieces, axis=1), jnp.concatenate(rows, axis=0), preferred_element_type=jnp.float32
        )
        where = pl.ds(half * 2 * BS, 2 * BS)
        acc[where, :] = term if first else acc[where, :] + term

    def contribute_step(step):
        for half in (0, 1):
            for way in (0, 1):
                if (step < half_z or half == way) and (step > 0 or way == 0):
                    s_pair_arrive(way, step, 2 * half)
                    s_pair_arrive(way, step, 2 * half + 1)
                    contribute(way, step, half, first=step == 0)

    virt_steps = [virt_arrived, virt_x_arrived]
    virt_steps += [functools.partial(virt_y_step, step) for step in range(1, half_y + 1)]
    done = 0
    for step in range(1, half_z + 1):
        for sub in range(AUX):
            ways = [way for way in (0, 1) if step < half_z or sub // 2 == way]
            for way in ways:
                s_arrive(way, step, sub)
                if step < half_z:
                    s_forward(way, step, sub)
            for way in ways:
                s_pair(way, step, sub)
        if step >= V_STEP and virt_steps:
            virt_steps.pop(0)()
    for virt_step in virt_steps:
        virt_step()
    while done <= half_z:
        contribute_step(done)
        done += 1

    tiles = acc[...].astype(jnp.bfloat16).astype(jnp.float32)
    sums = []
    for first in range(AUX):
        tile = tiles[first * BS:(first + 1) * BS, :]
        for second in range(AUX):
            sums.append(jnp.sum(tile * chosen[:, second * BS:(second + 1) * BS], axis=0, keepdims=True))
    total = jnp.sum(jnp.concatenate(sums, axis=0), axis=1, keepdims=True)
    pairs = lax.broadcasted_iota(jnp.int32, (AUX * AUX, BS), 0)
    lanes = lax.broadcasted_iota(jnp.int32, (AUX * AUX, BS), 1)
    message = jnp.sum(jnp.where(pairs == lanes, total, 0.0), axis=0, keepdims=True)

    def exchange(buffer, mine, members, stage, device_of, value):
        buffer[mine] = value

        def copy_to(slot, to):
            return pltpu.make_async_remote_copy(
                src_ref=buffer.at[slot], dst_ref=buffer.at[slot], send_sem=r_send.at[stage],
                recv_sem=r_recv.at[stage], device_id=device_of(to), device_id_type=MESH,
            )

        @pl.loop(0, members - 1)
        def _(turn):
            away = lax.div(turn + 1, 2)
            step = members // 2 + away * (1 - 2 * lax.rem(turn, 2))
            copy_to(mine, wrap(mine + step, members)).start()

        def everything():
            some = buffer.at[pl.ds(0, members - 1)]
            return pltpu.make_async_remote_copy(
                src_ref=some, dst_ref=some, send_sem=r_send.at[stage], recv_sem=r_recv.at[stage],
                device_id=device_of(mine), device_id_type=MESH,
            )

        return everything

    over_z = exchange(sum_z, blk, nb, 0, lambda to: (to, col), message)

    for aux in range(AUX):
        spread[pl.ds(aux, BS, stride=AUX), :] = tiles[aux * BS:(aux + 1) * BS, :]
    out_ref[...] = spread[...].T.astype(jnp.bfloat16)

    def all_sent(ref, sem):
        pltpu.make_async_remote_copy(
            src_ref=ref, dst_ref=ref, send_sem=sem.at[0], recv_sem=o_recv.at[0, 0], device_id=pair, device_id_type=MESH
        ).wait_send()

    all_sent(occ_all.at[pl.ds(0, nz - 1)], o_send)
    all_sent(occ_all.at[pl.ds(0, nz)], op_send)
    all_sent(s_all.at[pl.ds(0, nz - 1)], s_send)
    all_sent(s_all.at[pl.ds(0, nz)], sp_send)
    all_sent(virt_all.at[0, pl.ds(0, nx - 1)], vx_send)
    all_sent(virt_all.at[pl.ds(0, ny - 1)], vy_send)

    over_z().wait_recv()
    message = jnp.sum(sum_z[...], axis=0)
    over_col = exchange(sum_c, col, ny * nx, 1, lambda to: (blk, to), message)
    over_z().wait_send()
    over_col().wait_recv()
    message = jnp.sum(sum_c[...], axis=0)

    scale = 1.0 / (BS * math.sqrt(nb * n_stored))
    value = jnp.broadcast_to(message, (AUX, BS)) * scale
    lanes = lax.broadcasted_iota(jnp.int32, (AUX, BS), 1)
    firsts = lax.broadcasted_iota(jnp.int32, (AUX, BS), 0)
    place = lax.broadcasted_iota(jnp.int32, (AUX, AUX), 1)
    response = jnp.zeros((AUX, AUX), jnp.float32)
    for second in range(AUX):
        picked = jnp.sum(jnp.where(lanes == firsts * AUX + second, value, 0.0), axis=1, keepdims=True)
        response = response + jnp.where(place == second, picked, 0.0)
    resp_ref[...] = response
    over_col().wait_send()


def per_device(dims, three_center, block_rows, occupied, virtual):
    nz, ny, nx = dims
    nb = CORES * nz
    n_stored = three_center.shape[0]
    half_z, half_y = nz // 2, ny // 2
    any_space = pl.BlockSpec(memory_space=pl.ANY)
    vmem = pl.BlockSpec(memory_space=pltpu.VMEM)
    bf16, f32 = jnp.bfloat16, jnp.float32
    dma = pltpu.SemaphoreType.DMA
    return pl.pallas_call(
        functools.partial(kernel, dims),
        out_shape=(
            jax.ShapeDtypeStruct((BS, AUX * BS), bf16),
            jax.ShapeDtypeStruct((AUX, AUX), f32),
        ),
        in_specs=[pl.BlockSpec(memory_space=pltpu.SMEM), any_space, any_space, any_space],
        out_specs=(vmem, vmem),
        scratch_shapes=[
            pltpu.VMEM((BS, BS), bf16),
            pltpu.VMEM((n_stored * BS * AUX, BS), bf16),
            pltpu.VMEM((n_stored * BS * AUX, BS), f32),
            pltpu.VMEM((n_stored * BS, AUX * BS), bf16),
            pltpu.VMEM((BS, AUX * BS), f32),
            pltpu.VMEM((nb, BS, BS), bf16),
            pltpu.VMEM((nb, AUX, BS, BS), bf16),
            pltpu.VMEM((ny, nx, nb // nx, BS // ny, BS), bf16),
            pltpu.VMEM((AUX * BS, BS), f32),
            pltpu.VMEM((AUX * BS, BS), f32),
            pltpu.VMEM((nb, 1, BS), f32),
            pltpu.VMEM((ny * nx, 1, BS), f32),
            dma((2,)),
            dma((1,)), dma((2, half_z + 1)),
            dma((1,)), dma((2, half_z + 1)),
            dma((1,)), dma((2, half_z + 1, AUX)),
            dma((1,)), dma((2, half_z + 1, AUX)),
            dma((nb // nx,)), dma((nb // nx,)),
            dma((1,)), dma((nx,)),
            dma((1,)), dma((2, half_y + 1, 2)),
            dma((2,)), dma((2,)),
        ],
        compiler_params=pltpu.CompilerParams(
            collective_id=0, has_side_effects=True, vmem_limit_bytes=60 * 1024 * 1024
        ),
    )(block_rows, three_center.reshape(-1, BS), occupied, virtual)


def solution(mesh):
    in_specs = (P("blk", None, None, None), P("blk"), P("blk", "col"), P("blk", None))
    out_specs = (P("blk", "col"), P())
    return jax.shard_map(
        functools.partial(per_device, DIMS), mesh=mesh, in_specs=in_specs, out_specs=out_specs, check_vma=False
    )
```

time: 110 us -> 94.1 us (0.86)
  Pallas kernels: 104 us -> 91.1 us
  local copies, waits for them, and re-layouts: 5.09 us -> 2.15 us
    pallas_call x1, Pallas kernels: 104 us -> 91.1 us  [per_device(): pl.pallas_call(functools.partial(kernel, dims), out_shape=(jax.ShapeDtype...]
    unnamed x10 -> x4, local copies, waits for them, and re-layouts: 5.09 us -> 2.15 us
where the time goes in v2:
time: 94.1 us; the launch traced here: 93.9 us
  Pallas kernels  91.1 us (97%)
  local copies, waits for them, and re-layouts  2.15 us (2%)
    pallas_call x1, Pallas kernels, per_device(): pl.pallas_call(functools.partial(kernel, dims), out_shape=(jax.ShapeDtype...  91.1 us
    unnamed x4, local copies, waits for them, and re-layouts  2.15 us

profile of v2, /device:TPU:1, one launch (start us, length us, event | category | flops | bytes accessed | tf_op | source)
XLA Modules:
  0.0 93.9 jit_solution(17344337939309107036)
XLA Ops:
  0.6 91.1 %shard_map.59 = (bf16[128,512]{1,0:T(8,128)(2,1)}, f32[4,4]{1,0:T(4,128)}) custom-call(s32[8]{0:T(128)} %rows_ref.1, bf16[4096,128]{1,0:T(8,128)(2,1)} %bitcast.1, bf16[128,128]{1,0:T(8,128)(2,1)} %occ_hbm.1, bf16[128,4096]{1,0:T(8,128)(2,1)} %virt_hbm.1), custom_call_target="tpu_custom_call" | custom-call | tf_op jit(solution)/shard_map/pallas_call | solution.py:357
  91.7 0.0 copy-start
  91.7 1.6 %copy.8 = bf16[128,512]{1,0:T(8,128)(2,1)} copy(bf16[128,512]{1,0:T(8,128)(2,1)} %get-tuple-element.4) | data formatting | bytes 262144
  93.3 0.0 copy-done
  93.3 0.6 copy.9
Async XLA Ops:
  91.7 1.6 %copy-start = (f32[4,4]{1,0:T(4,128)S(1)}, f32[4,4]{1,0:T(4,128)}, u32[]{:S(2)}) copy-start(f32[4,4]{1,0:T(4,128)} %get-tuple-element.5) | copy-start | bytes 196

commit v3 on v2

--- a/solution.py
+++ b/solution.py
@@ -13,14 +13,14 @@
 CORES = 2
 DIMS = (16, 8, 4)
 MESH = pl.DeviceIdType.MESH
-V_STEP = 2
+VIRT_AT = (1, 3, 5, 6)
 OCC_FROM = {1: 0, 2: 0, 3: 0, 4: 3, 5: 3, 6: 3, 7: 6, 8: 6}
 
 
 def kernel(
     dims, rows_ref, blocks_hbm, occ_hbm, virt_hbm, out_ref, resp_ref,
-    occ_in, blocks_in, wide, blocks, chosen, occ_all, s_all, virt_all, acc, spread, sum_z, sum_c,
-    in_sem, o_send, o_recv, op_send, op_recv, s_send, s_recv, sp_send, sp_recv,
+    occ_in, blocks_in, wide, blocks, chosen, occ_low, occ_high, s_all, virt_all, acc, spread, sum_z, sum_c,
+    in_sem, o_send, o_recv, op_send, op_recv, s_send, s_recv, sp_send, sp_recv, so_recv,
     vz_send, vz_recv, vx_send, vx_recv, vy_send, vy_recv, r_send, r_recv,
 ):
     nz, ny, nx = dims
@@ -51,13 +51,14 @@
     load_blocks.start()
 
     barrier = pltpu.get_barrier_semaphore()
-    near_z = [hops for hops in sorted({reach - start for reach, start in OCC_FROM.items()}) if hops <= half_z]
-    greeted = [(at_z(sign * hops), col) for hops in near_z for sign in (1, -1)] + [pair, up, down]
+    greeted = [(wrap(blk + step, nb), col) for step in range(1, nb)] + [up, down]
     greeted += [(blk, y * nx + wrap(x + step, nx)) for step in range(1, nx)]
     for device in greeted:
         pl.semaphore_signal(barrier, inc=1, device_id=device, device_id_type=MESH)
     load_occ.wait()
-    occ_all[blk] = occ_in[...].T
+    turned = occ_in[...].T
+    occ_low[blk] = turned[:BS // 2]
+    occ_high[blk] = turned[BS // 2:]
     pl.semaphore_wait(barrier, len(greeted))
 
     def send(src, dst, send_sem, recv_sem, to):
@@ -71,34 +72,47 @@
             src_ref=ref, dst_ref=ref, send_sem=send_sem, recv_sem=recv_sem, device_id=source, device_id_type=MESH
         ).wait_recv()
 
-    def occ_view(way, step, part, which=None):
-        index = at_z(-step if way == 0 else step, which)
-        if part < half_z:
-            return occ_all.at[index]
-        return occ_all.at[index, pl.ds(way * (BS // 2), BS // 2)]
-
-    def occ_forward(way, step):
+    occ = (occ_low, occ_high)
+
+    def occ_view(half, way, step, which=None):
+        return occ[half].at[at_z(-step if way == 0 else step, which)]
+
+    def occ_forward(half, way, step):
         for reach in range(half_z, step, -1):
-            if OCC_FROM[reach] == step:
-                view = occ_view(way, step, reach)
+            if OCC_FROM[reach] == step and (reach < half_z or way == half):
+                view = occ_view(half, way, step)
                 hops = reach - step
-                send(view, view, o_send.at[0], o_recv.at[way, reach], (at_z(hops if way == 0 else -hops), col))
-
-    def occ_pair(way, step):
-        view = occ_view(way, step, step)
-        send(view, view, op_send.at[0], op_recv.at[way, step], pair)
-
-    def occ_arrive(way, step):
-        hops = step - OCC_FROM[step]
-        arrive(occ_view(way, step, step), o_send.at[0], o_recv.at[way, step],
-               (at_z(-hops if way == 0 else hops), col))
-
-    def occ_pair_arrive(way, step):
-        arrive(occ_view(way, step, step, 1 - core), op_send.at[0], op_recv.at[way, step], pair)
-
-    occ_forward(0, 0)
-    occ_forward(1, 0)
-    occ_pair(0, 0)
+                send(view, view, o_send.at[half], o_recv.at[half, way, reach], (at_z(hops if way == 0 else -hops), col))
+
+    def occ_pair(half, way, step):
+        view = occ_view(half, way, step)
+        send(view, view, op_send.at[half], op_recv.at[half, way, step], pair)
+
+    def occ_steps(half, first, last):
+        for step in range(first, min(last, half_z) + 1):
+            ways = [way for way in (0, 1) if step < half_z or way == half]
+            for way in ways:
+                hops = step - OCC_FROM[step]
+                arrive(occ_view(half, way, step), o_send.at[half], o_recv.at[half, way, step],
+                       (at_z(-hops if way == 0 else hops), col))
+                occ_forward(half, way, step)
+            for way in ways:
+                occ_pair(half, way, step)
+
+    def occ_pair_arrive(half, way, step):
+        arrive(occ_view(half, way, step, 1 - core), op_send.at[half], op_recv.at[half, way, step], pair)
+
+    def occ_whole(half):
+        occ_pair_arrive(half, 0, 0)
+        for step in range(1, half_z + 1):
+            for way in (0, 1):
+                if step < half_z or way == half:
+                    occ_pair_arrive(half, way, step)
+
+    for half in (0, 1):
+        occ_forward(half, 0, 0)
+        occ_forward(half, 1, 0)
+        occ_pair(half, 0, 0)
 
     def virt_part(part):
         return virt_all.at[y, x, part]
@@ -128,6 +142,7 @@
         for part in range(1, n_part):
             virt_remote(part).start()
 
+    virt_start()
     load_blocks.wait()
 
     def order_blocks(index):
@@ -180,102 +195,121 @@
 
     for index in range(n_stored):
         order_blocks(index)
-    for step in range(1, half_z + 1):
-        for way in (0, 1):
-            occ_arrive(way, step)
-            if step < half_z:
-                occ_forward(way, step)
-        for way in (0, 1):
-            occ_pair(way, step)
-    occ_pair_arrive(0, 0)
-    for step in range(1, half_z + 1):
-        for way in (0, 1):
-            occ_pair_arrive(way, step)
-
-    def s_view(way, step, sub, which=None):
-        return s_all.at[at_z(-step if way == 0 else step, which), sub]
-
-    def s_forward(way, step, sub):
-        if step + 1 < half_z or sub // 2 == way:
-            view = s_view(way, step, sub)
-            send(view, view, s_send.at[0], s_recv.at[way, step + 1, sub], right if way == 0 else left)
-
-    def s_pair(way, step, sub):
-        view = s_view(way, step, sub)
-        send(view, view, sp_send.at[0], sp_recv.at[way, step, sub], pair)
-
-    def s_arrive(way, step, sub):
-        arrive(s_view(way, step, sub), s_send.at[0], s_recv.at[way, step, sub],
-               left if way == 0 else right)
-
-    def s_pair_arrive(way, step, sub):
-        arrive(s_view(way, step, sub, 1 - core), sp_send.at[0], sp_recv.at[way, step, sub], pair)
-
-    occ_rows = jnp.concatenate([occ_all[rows_ref[index]] for index in range(n_stored)], axis=1)
-    for half in (0, 1):
-        sums = jnp.dot(
-            occ_rows, blocks[:, half * 2 * BS:(half + 1) * 2 * BS], preferred_element_type=jnp.float32
-        ).astype(jnp.bfloat16)
+    for first, last in ((1, 3), (4, 6)):
+        for half in (0, 1):
+            occ_steps(half, first, last)
+
+    sign = 1 - 2 * core
+    onward, behind = (at_z(sign), col), (at_z(-sign), col)
+    order = [lax.rem(2 * core + turn, AUX) for turn in range(AUX)]
+
+    def s_onward(base, which, step, sub):
+        view = s_all.at[base * CORES + which, sub]
+        send(view, view, s_send.at[0], s_recv.at[step, which, sub], onward)
+
+    def s_pair(base, which, step, sub):
+        view = s_all.at[base * CORES + which, sub]
+        send(view, view, sp_send.at[0], sp_recv.at[step, lax.div(sub, 2)], pair)
+
+    def s_pair_arrive(base, step, half):
+        arrive(s_all.at[pl.ds(base * CORES, CORES), pl.ds(2 * half, 2)], sp_send.at[0], sp_recv.at[step, half], pair)
+
+    def s_step(step):
+        base = wrap(z - sign * step, nz)
+        for which in (core, 1 - core):
+            for turn, sub in enumerate(order if step + 1 >= half_z else range(AUX)):
+                if step < half_z or turn < 2:
+                    view = s_all.at[base * CORES + which, sub]
+                    arrive(view, s_send.at[0], s_recv.at[step, which, sub], behind)
+                    if step + 1 < half_z or (step + 1 == half_z and turn < 2):
+                        s_onward(base, which, step + 1, sub)
+                    s_pair(base, which, step, sub)
+
+    def s_first(half):
+        occ_rows = jnp.concatenate([occ[half][rows_ref[index]] for index in range(n_stored)], axis=1)
+        sums = jnp.dot(occ_rows, blocks[...], preferred_element_type=jnp.float32).astype(jnp.bfloat16)
+        for aux in range(AUX):
+            s_all[blk, 2 * half + aux // 2, aux % 2] = sums[:, aux * BS:(aux + 1) * BS]
         for sub in (2 * half, 2 * half + 1):
-            s_all[blk, sub] = sums[:, (sub % 2) * BS:(sub % 2 + 1) * BS]
-            s_forward(0, 0, sub)
-            s_forward(1, 0, sub)
+            s_onward(z, core, 1, sub)
+            view = s_all.at[blk, sub]
+            send(view, view, sp_send.at[0], so_recv.at[sub], pair)
+
+    def s_first_pair(half):
         for sub in (2 * half, 2 * half + 1):
-            s_pair(0, 0, sub)
-    virt_start()
-
+            arrive(s_all.at[z * CORES + 1 - core, sub], sp_send.at[0], so_recv.at[sub], pair)
+            s_onward(z, 1 - core, 1, sub)
+
+    virt_arrived()
+    occ_steps(0, 7, half_z)
+    occ_whole(0)
+    s_first(0)
+    virt_x_arrived()
+    occ_steps(1, 7, half_z)
+    s_first_pair(0)
+    occ_whole(1)
+    s_first(1)
+    s_first_pair(1)
     picked = jnp.zeros((BS, AUX * BS), jnp.float32)
     for index in range(n_stored):
         here = (rows_ref[index] == col).astype(jnp.float32)
         picked = picked + blocks[index * BS:(index + 1) * BS, :].astype(jnp.float32) * here
     chosen[...] = picked
 
-    def contribute(way, step, half, first=False):
-        base = wrap(z - step if way == 0 else z + step, nz)
+    def contribute(base, half=None, first=False):
         pieces, rows = [], []
         for which in range(CORES):
             index = base * CORES + which
-            pieces.append(s_all[index, 2 * half:2 * half + 2].reshape(2 * BS, BS))
+            if half is None:
+                pieces.append(s_all[index].reshape(AUX * BS, BS))
+            else:
+                pieces.append(s_all[index, pl.ds(2 * half, 2)].reshape(2 * BS, BS))
             away = wrap(blk - index, nb)
             rows.append(virt_all[:, lax.rem(away, nx), lax.div(away, nx)].reshape(BS, BS))
         term = jnp.dot(
             jnp.concatenate(pieces, axis=1), jnp.concatenate(rows, axis=0), preferred_element_type=jnp.float32
         )
-        where = pl.ds(half * 2 * BS, 2 * BS)
+        where = slice(None) if half is None else pl.ds(pl.multiple_of(half * 2 * BS, 2 * BS), 2 * BS)
         acc[where, :] = term if first else acc[where, :] + term
 
     def contribute_step(step):
-        for half in (0, 1):
-            for way in (0, 1):
-                if (step < half_z or half == way) and (step > 0 or way == 0):
-                    s_pair_arrive(way, step, 2 * half)
-                    s_pair_arrive(way, step, 2 * half + 1)
-                    contribute(way, step, half, first=step == 0)
-
-    virt_steps = [virt_arrived, virt_x_arrived]
-    virt_steps += [functools.partial(virt_y_step, step) for step in range(1, half_y + 1)]
+        mine, other = wrap(z - sign * step, nz), wrap(z + sign * step, nz)
+        if step == half_z:
+            contribute(mine, core)
+            s_pair_arrive(other, step, 1 - core)
+            contribute(other, 1 - core)
+            return
+        contribute(mine, first=step == 0)
+        if step > 0:
+            for half in (0, 1):
+                s_pair_arrive(other, step, half)
+            contribute(other)
+
+    virt_steps = [functools.partial(virt_y_step, step) for step in range(1, half_y + 1)]
     done = 0
     for step in range(1, half_z + 1):
-        for sub in range(AUX):
-            ways = [way for way in (0, 1) if step < half_z or sub // 2 == way]
-            for way in ways:
-                s_arrive(way, step, sub)
-                if step < half_z:
-                    s_forward(way, step, sub)
-            for way in ways:
-                s_pair(way, step, sub)
-        if step >= V_STEP and virt_steps:
+        s_step(step)
+        if step in VIRT_AT and virt_steps:
             virt_steps.pop(0)()
+        if not virt_steps and VIRT_AT[-1] < step < half_z:
+            for _ in range(4):
+                contribute_step(done)
+                done += 1
     for virt_step in virt_steps:
         virt_step()
     while done <= half_z:
         contribute_step(done)
         done += 1
 
-    tiles = acc[...].astype(jnp.bfloat16).astype(jnp.float32)
+    held = acc[...].astype(jnp.bfloat16).astype(jnp.float32)
+    span = BS // 2
+    tiles = [
+        jnp.concatenate([held[(half * AUX + aux) * span:(half * AUX + aux + 1) * span] for half in (0, 1)], axis=0)
+        for aux in range(AUX)
+    ]
     sums = []
     for first in range(AUX):
-        tile = tiles[first * BS:(first + 1) * BS, :]
+        tile = tiles[first]
         for second in range(AUX):
             sums.append(jnp.sum(tile * chosen[:, second * BS:(second + 1) * BS], axis=0, keepdims=True))
     total = jnp.sum(jnp.concatenate(sums, axis=0), axis=1, keepdims=True)
@@ -310,16 +344,17 @@
     over_z = exchange(sum_z, blk, nb, 0, lambda to: (to, col), message)
 
     for aux in range(AUX):
-        spread[pl.ds(aux, BS, stride=AUX), :] = tiles[aux * BS:(aux + 1) * BS, :]
+        spread[pl.ds(aux, BS, stride=AUX), :] = tiles[aux]
     out_ref[...] = spread[...].T.astype(jnp.bfloat16)
 
-    def all_sent(ref, sem):
+    def all_sent(ref, sem, index=0):
         pltpu.make_async_remote_copy(
-            src_ref=ref, dst_ref=ref, send_sem=sem.at[0], recv_sem=o_recv.at[0, 0], device_id=pair, device_id_type=MESH
+            src_ref=ref, dst_ref=ref, send_sem=sem.at[index], recv_sem=o_recv.at[0, 0, 0], device_id=pair, device_id_type=MESH
         ).wait_send()
 
-    all_sent(occ_all.at[pl.ds(0, nz - 1)], o_send)
-    all_sent(occ_all.at[pl.ds(0, nz)], op_send)
+    for half in (0, 1):
+        all_sent(occ[half].at[pl.ds(0, nz - 1)], o_send, half)
+        all_sent(occ[half].at[pl.ds(0, nz)], op_send, half)
     all_sent(s_all.at[pl.ds(0, nz - 1)], s_send)
     all_sent(s_all.at[pl.ds(0, nz)], sp_send)
     all_sent(virt_all.at[0, pl.ds(0, nx - 1)], vx_send)
@@ -350,7 +385,7 @@
     nb = CORES * nz
     n_stored = three_center.shape[0]
     half_z, half_y = nz // 2, ny // 2
-    any_space = pl.BlockSpec(memory_space=pl.ANY)
+    in_hbm = pl.BlockSpec(memory_space=pl.ANY)
     vmem = pl.BlockSpec(memory_space=pltpu.VMEM)
     bf16, f32 = jnp.bfloat16, jnp.float32
     dma = pltpu.SemaphoreType.DMA
@@ -360,7 +395,7 @@
             jax.ShapeDtypeStruct((BS, AUX * BS), bf16),
             jax.ShapeDtypeStruct((AUX, AUX), f32),
         ),
-        in_specs=[pl.BlockSpec(memory_space=pltpu.SMEM), any_space, any_space, any_space],
+        in_specs=[pl.BlockSpec(memory_space=pltpu.SMEM), in_hbm, in_hbm, in_hbm],
         out_specs=(vmem, vmem),
         scratch_shapes=[
             pltpu.VMEM((BS, BS), bf16),
@@ -368,18 +403,19 @@
             pltpu.VMEM((n_stored * BS * AUX, BS), f32),
             pltpu.VMEM((n_stored * BS, AUX * BS), bf16),
             pltpu.VMEM((BS, AUX * BS), f32),
-            pltpu.VMEM((nb, BS, BS), bf16),
-            pltpu.VMEM((nb, AUX, BS, BS), bf16),
+            pltpu.VMEM((nb, BS // 2, BS), bf16),
+            pltpu.VMEM((nb, BS // 2, BS), bf16),
+            pltpu.VMEM((nb, AUX, 2, BS // 2, BS), bf16),
             pltpu.VMEM((ny, nx, nb // nx, BS // ny, BS), bf16),
             pltpu.VMEM((AUX * BS, BS), f32),
             pltpu.VMEM((AUX * BS, BS), f32),
             pltpu.VMEM((nb, 1, BS), f32),
             pltpu.VMEM((ny * nx, 1, BS), f32),
             dma((2,)),
-            dma((1,)), dma((2, half_z + 1)),
-            dma((1,)), dma((2, half_z + 1)),
-            dma((1,)), dma((2, half_z + 1, AUX)),
-            dma((1,)), dma((2, half_z + 1, AUX)),
+            dma((2,)), dma((2, 2, half_z + 1)),
+            dma((2,)), dma((2, 2, half_z + 1)),
+            dma((1,)), dma((half_z + 1, CORES, AUX)),
+            dma((1,)), dma((half_z + 1, 2)), dma((AUX,)),
             dma((nb // nx,)), dma((nb // nx,)),
             dma((1,)), dma((nx,)),
             dma((1,)), dma((2, half_y + 1, 2)),

time: 94.1 us -> 87.7 us (0.932)
  Pallas kernels: 91.1 us -> 84.8 us
    pallas_call x1, Pallas kernels: 91.1 us -> 84.8 us  [per_device(): pl.pallas_call(functools.partial(kernel, dims), out_shape=(jax.ShapeDtype...]
where the time goes in v3:
time: 87.7 us; the launch traced here: 87.6 us
  Pallas kernels  84.8 us (97%)
  local copies, waits for them, and re-layouts  2.15 us (2%)
    pallas_call x1, Pallas kernels, per_device(): pl.pallas_call(functools.partial(kernel, dims), out_shape=(jax.ShapeDtype...  84.8 us
    unnamed x4, local copies, waits for them, and re-layouts  2.15 us

profile of v3, /device:TPU:1, one launch (start us, length us, event | category | flops | bytes accessed | tf_op | source)
XLA Modules:
  0.0 87.6 jit_solution(12794155523781794619)
XLA Ops:
  0.6 84.8 %shard_map.59 = (bf16[128,512]{1,0:T(8,128)(2,1)}, f32[4,4]{1,0:T(4,128)}) custom-call(s32[8]{0:T(128)} %rows_ref.1, bf16[4096,128]{1,0:T(8,128)(2,1)} %bitcast.1, bf16[128,128]{1,0:T(8,128)(2,1)} %occ_hbm.1, bf16[128,4096]{1,0:T(8,128)(2,1)} %virt_hbm.1), custom_call_target="tpu_custom_call" | custom-call | tf_op jit(solution)/shard_map/pallas_call | solution.py:392
  85.4 0.0 copy-start
  85.4 1.6 %copy.8 = bf16[128,512]{1,0:T(8,128)(2,1)} copy(bf16[128,512]{1,0:T(8,128)(2,1)} %get-tuple-element.4) | data formatting | bytes 262144
  87.0 0.0 copy-done
  87.0 0.6 copy.9
Async XLA Ops:
  85.4 1.6 %copy-start = (f32[4,4]{1,0:T(4,128)S(1)}, f32[4,4]{1,0:T(4,128)}, u32[]{:S(2)}) copy-start(f32[4,4]{1,0:T(4,128)} %get-tuple-element.5) | copy-start | bytes 196

commit v4 on v3

--- a/solution.py
+++ b/solution.py
@@ -207,9 +207,9 @@
         view = s_all.at[base * CORES + which, sub]
         send(view, view, s_send.at[0], s_recv.at[step, which, sub], onward)
 
-    def s_pair(base, which, step, sub):
-        view = s_all.at[base * CORES + which, sub]
-        send(view, view, sp_send.at[0], sp_recv.at[step, lax.div(sub, 2)], pair)
+    def s_pair(base, which, step, half):
+        view = s_all.at[base * CORES + which, pl.ds(2 * half, 2)]
+        send(view, view, sp_send.at[0], sp_recv.at[step, half], pair)
 
     def s_pair_arrive(base, step, half):
         arrive(s_all.at[pl.ds(base * CORES, CORES), pl.ds(2 * half, 2)], sp_send.at[0], sp_recv.at[step, half], pair)
@@ -223,7 +223,8 @@
                     arrive(view, s_send.at[0], s_recv.at[step, which, sub], behind)
                     if step + 1 < half_z or (step + 1 == half_z and turn < 2):
                         s_onward(base, which, step + 1, sub)
-                    s_pair(base, which, step, sub)
+                    if turn % 2 == 1:
+                        s_pair(base, which, step, lax.div(sub, 2))
 
     def s_first(half):
         occ_rows = jnp.concatenate([occ[half][rows_ref[index]] for index in range(n_stored)], axis=1)

time: 87.7 us -> 87.7 us (level)
  no operation moved by 1% of the time
where the time goes in v4:
time: 87.7 us; the launch traced here: 87.6 us
  Pallas kernels  84.8 us (97%)
  local copies, waits for them, and re-layouts  2.15 us (2%)
    pallas_call x1, Pallas kernels, per_device(): pl.pallas_call(functools.partial(kernel, dims), out_shape=(jax.ShapeDtype...  84.8 us
    unnamed x4, local copies, waits for them, and re-layouts  2.15 us

profile of v4, /device:TPU:1, one launch (start us, length us, event | category | flops | bytes accessed | tf_op | source)
XLA Modules:
  0.0 87.6 jit_solution(10343427023250036203)
XLA Ops:
  0.6 84.8 %shard_map.59 = (bf16[128,512]{1,0:T(8,128)(2,1)}, f32[4,4]{1,0:T(4,128)}) custom-call(s32[8]{0:T(128)} %rows_ref.1, bf16[4096,128]{1,0:T(8,128)(2,1)} %bitcast.1, bf16[128,128]{1,0:T(8,128)(2,1)} %occ_hbm.1, bf16[128,4096]{1,0:T(8,128)(2,1)} %virt_hbm.1), custom_call_target="tpu_custom_call" | custom-call | tf_op jit(solution)/shard_map/pallas_call | solution.py:393
  85.4 0.0 copy-start
  85.4 1.6 %copy.8 = bf16[128,512]{1,0:T(8,128)(2,1)} copy(bf16[128,512]{1,0:T(8,128)(2,1)} %get-tuple-element.4) | data formatting | bytes 262144
  87.0 0.0 copy-done
  87.0 0.6 copy.9
Async XLA Ops:
  85.4 1.6 %copy-start = (f32[4,4]{1,0:T(4,128)S(1)}, f32[4,4]{1,0:T(4,128)}, u32[]{:S(2)}) copy-start(f32[4,4]{1,0:T(4,128)} %get-tuple-element.5) | copy-start | bytes 196
